TPU v7x, 512 devices: a whole 4x8x8 slice. The times are simulated.
512 devices in a mesh: ctx: 128 (over y, z, core), head: 4 (over x).
Axes of the slice: x: 4, y: 8, z: 8, core: 2. Of those that a mesh axis runs over, the one named last changes fastest.
Arguments:
- queries: bfloat16 [3, 8, 8192], P(None, None, 'head'), may hold values from -8 to 8
- k_cache: bfloat16 [8, 32768, 1024], P(None, 'ctx', 'head'), may hold values from -6 to 6
- v_cache: bfloat16 [8, 32768, 1024], P(None, 'ctx', 'head'), may hold values from -6 to 6
- new_keys: bfloat16 [3, 8, 1024], P(None, None, 'head'), may hold values from -6 to 6
- new_values: bfloat16 [3, 8, 1024], P(None, None, 'head'), may hold values from -6 to 6
- fill: int32 [8, 128], P(None, 'ctx'), may hold values from 2 to 253, as said below
- owner: int32 [3, 8], replicated, may hold values from 0 to 127
- out_weight: bfloat16 [8192, 8192], P('head', 'ctx'), may hold values from -0.25 to 0.25
Outputs:
- keys_out: bfloat16 [8, 32768, 1024], P(None, 'ctx', 'head')
- values_out: bfloat16 [8, 32768, 1024], P(None, 'ctx', 'head')
- mixed: bfloat16 [3, 8, 8192], P(None, None, ('ctx', 'head'))
Inputs may be any that keep to these rules, and one draw needn't show every extreme that they name: Rows 0 to fill - 1 of each shard hold the sequence's earlier positions; some entry equals 253.
All inputs are finite; a program needn't handle non-finite values.
Results may differ from a plain program's by a relative error of at most 0.0051.
Values may be sent and summed in bfloat16 or wider, within the bound.
No kernel may reach another device: no remote copies, remote signals or barrier semaphores. Data moves between devices by JAX's collectives and lax.ppermute only.
A program may use at most 128 MiB of HBM per device.

v0:
```python
import jax
import jax.numpy as jnp
from jax import lax
from jax.sharding import PartitionSpec as P

HD = 128


def on_device(queries, k_cache, v_cache, new_keys, new_values, fill, owner, out_weight):
    steps, batch = owner.shape
    rows = k_cache.shape[1]
    device_pos = lax.axis_index("ctx")
    mine = (owner == device_pos).astype(jnp.int32)
    seen = jnp.cumsum(mine, axis=0)
    local_fill = fill[:, 0]
    slot = local_fill[None, :] + seen - 1
    row_ids = lax.broadcasted_iota(jnp.int32, (batch, rows), 1)
    keys_out, values_out = (k_cache, v_cache)
    for step in range(steps):
        target = ((row_ids == slot[step][:, None]) & (mine[step][:, None] == 1))[:, :, None]
        keys_out = jnp.where(target, new_keys[step][:, None, :], keys_out)
        values_out = jnp.where(target, new_values[step][:, None, :], values_out)
    lengths = local_fill[None, :] + seen
    kv_local = keys_out.shape[2] // HD
    groups = queries.shape[2] // (kv_local * HD)
    query_heads = queries.reshape(steps, batch, kv_local, groups, HD)
    key_heads = keys_out.reshape(batch, rows, kv_local, HD)
    value_heads = values_out.reshape(batch, rows, kv_local, HD)
    scores = jnp.einsum(
        "sbgqd,brgd->sbgqr", query_heads, key_heads, preferred_element_type=jnp.float32
    ) * (1.0 / HD**0.5)
    slot_ids = lax.broadcasted_iota(jnp.int32, (1, 1, 1, 1, rows), 4)
    live = slot_ids < lengths[:, :, None, None, None]
    masked = jnp.where(live, scores, -1e30)
    peak = jnp.max(masked, axis=-1)
    weights = jnp.where(live, jnp.exp(masked - peak[..., None]), 0.0)
    total = jnp.sum(weights, axis=-1)
    rounded = weights.astype(jnp.bfloat16)
    numer = jnp.einsum(
        "sbgqr,brgd->sbgqd", rounded, value_heads, preferred_element_type=jnp.float32
    )
    largest = lax.pmax(peak, "ctx")
    factor = jnp.exp(peak - largest)
    numer_all, total_all = lax.psum((numer * factor[..., None], total * factor), "ctx")
    attention = (numer_all / total_all[..., None]).astype(jnp.bfloat16)
    attention_rows = attention.reshape(steps * batch, kv_local * groups * HD)
    partial_out = jnp.dot(attention_rows, out_weight, preferred_element_type=jnp.float32)
    mixed = lax.psum_scatter(partial_out, "head", scatter_dimension=1, tiled=True).astype(
        jnp.bfloat16
    )
    return (keys_out, values_out, mixed.reshape(steps, batch, -1))


def solution(mesh):
    in_specs = (
        P(None, None, "head"),
        P(None, "ctx", "head"),
        P(None, "ctx", "head"),
        P(None, None, "head"),
        P(None, None, "head"),
        P(None, "ctx"),
        P(),
        P("head", "ctx"),
    )
    out_specs = (P(None, "ctx", "head"), P(None, "ctx", "head"), P(None, None, ("ctx", "head")))
    return jax.shard_map(
        on_device, mesh=mesh, in_specs=in_specs, out_specs=out_specs, check_vma=False
    )
```

profile of v0, /device:TPU:1, one launch (start us, length us, event | category | flops | bytes accessed | tf_op | source)
XLA Modules:
  0.0 1036.7 jit_solution(5860745015012057789)
XLA Ops:
  7.2 0.0 copy-start
  7.2 0.0 all-reduce.2.cloned.1.call-start
  7.2 0.7 copy-done.7
  8.0 0.0 copy-start.5
  8.0 0.0 copy-start.6
  8.0 0.6 copy-done.8
  8.6 0.1 fusion.14
  8.7 0.1 fusion.12
  8.8 3.0 select_select_fusion
  11.8 0.0 copy-start.2
  11.8 0.0 copy-start.1
  11.8 0.0 copy-start.9
  11.8 0.3 reshape.192
  12.1 0.6 copy-done.2
  12.7 0.1 copy.16
  12.8 0.1 iota_compare_fusion
  12.9 0.0 copy-done.9
  12.9 0.5 fusion.17
  13.4 498.1 %pmax.7 = f32[3,8,2,8]{3,0,2,1:T(4,128)S(1)} all-reduce(f32[3,8,2,8]{3,0,2,1:T(4,128)S(1)} %get-tuple-element.24), channel_id=1, replica_groups=mesh['ctx'=128,'head'=4] {'ctx'}, use_global_device_ids=true, to_apply=%region_2.3 | all-reduce | flops 384 | bytes 3072 | tf_op jit(solution)/shard_map/pmax | solution.py:42
  511.5 0.3 fusion.5
  511.7 0.3 reshape.191
  512.1 0.7 copy-done.4
  512.7 1.0 fusion.2
  513.7 0.0 all-reduce.2.cloned.1.call-update
  513.8 0.0 reduce-scatter.2.cloned.1.call-start
  513.8 490.9 %psum.15 = f32[3,8,2,8]{3,0,2,1:T(4,128)S(1)} all-reduce(f32[3,8,2,8]{3,0,2,1:T(4,128)S(1)} %get-tuple-element.6), channel_id=1, replica_groups=mesh['ctx'=128,'head'=4] {'ctx'}, use_global_device_ids=true, to_apply=%region_5.6 | all-reduce | flops 384 | bytes 3072 | tf_op jit(solution)/shard_map/psum | solution.py:44
  1004.7 1.0 divide_convert_fusion
  1005.9 0.8 fusion.18
  1006.7 0.0 reduce-scatter.2.cloned.1.call-update
  1006.7 21.8 %reduce-scatter.2.cloned.1.call-done = f32[24,16]{0,1:T(8,128)} async-done(((f32[24,64]{0,1:T(8,128)}), f32[24,16]{0,1:T(8,128)}) %reduce-scatter.2.cloned.1.call-update) | async-done | bytes 1552 | tf_op jit(solution)/shard_map/reduce_scatter | solution.py:48
  1028.5 0.7 convert_element_type.15
  1029.2 0.7 copy.21
  (19 shorter events, 0.2 us)
Async XLA Ops:
  7.2 998.7 %copy-start = (bf16[2048,64]{0,1:T(8,128)(2,1)S(1)}, bf16[2048,64]{0,1:T(8,128)(2,1)}, u32[]{:S(2)}) copy-start(bf16[2048,64]{0,1:T(8,128)(2,1)} %param.15) | copy-start | bytes 786436
  7.2 997.5 %all-reduce.2.cloned.1.call-start = ((), (), s32[]{:S(2)}) async-start(), calls=%async_computation.1 | async-start | bytes 393216 | tf_op jit(solution)/shard_map/psum | solution.py:44
  7.2 0.7 copy-start.7
  7.9 0.7 copy-start.8
  8.0 0.7 copy-start.5
  8.0 0.7 copy-start.6
  11.8 1.0 copy-start.2
  11.8 500.0 %copy-start.1 = (bf16[8,256,256]{2,1,0:T(8,128)(2,1)}, bf16[8,256,256]{2,1,0:T(8,128)(2,1)S(1)}, u32[]{:S(2)}) copy-start(bf16[8,256,256]{2,1,0:T(8,128)(2,1)S(1)} %get-tuple-element.16) | copy-start | bytes 3145732
  11.8 1.1 copy-start.9
  13.4 498.3 %copy-start.3 = (f32[3,8,2,8,256]{4,3,0,2,1:T(8,128)}, f32[3,8,2,8,256]{4,3,0,2,1:T(8,128)S(1)}, u32[]{:S(2)}) copy-start(f32[3,8,2,8,256]{4,3,0,2,1:T(8,128)S(1)} %get-tuple-element.25) | copy-start | bytes 1179652
  511.7 1.0 copy-start.4
  513.8 514.7 %reduce-scatter.2.cloned.1.call-start = ((), (), s32[]{:S(2)}) async-start(), calls=%async_computation.2 | async-start | bytes 40960 | tf_op jit(solution)/shard_map/reduce_scatter | solution.py:48
Sparse Core Ops, SparseCore 0:
  513.9 186.3 all-reduce.1
  1006.8 21.6 reduce-scatter.1
where the time goes:
time: 1040 us
  blocking collectives  989 us (95%)
  waiting for transfers between devices  21.8 us (2%)
  between operations  14.2 us (1%)
    pmax x1, blocking collectives, on_device(): largest = lax.pmax(peak, 'ctx')  498 us
    psum x1, blocking collectives, on_device(): lax.psum((numer * factor[..., None], total * factor), 'ctx')  491 us
    reduce_scatter x1, waiting for transfers between devices, on_device(): lax.psum_scatter(partial_out, 'head', scatter_dimension=1, tiled=True)  21.8 us
  transfers between devices with their start and end apart: 2, of which 1 were waited for; matrix products, arithmetic and copies ran while one was open for 0% of the time, Pallas kernels for 0%

commit v1 on v0

v1 whole, which is shorter than its diff:
```python
import functools

import jax
import jax.numpy as jnp
from jax import lax
from jax.experimental import pallas as pl
from jax.experimental.pallas import tpu as pltpu
from jax.sharding import Mesh
from jax.sharding import PartitionSpec as P

HD = 128
F32 = jnp.float32
BF16 = jnp.bfloat16
ATTEND_VMEM = 63_000_000
CTX = ("y", "z", "core")


def three_way(x):
    first = x.astype(BF16).astype(F32)
    rest = x - first
    second = rest.astype(BF16).astype(F32)
    return first, second, rest - second


def stat_rows(peak, total):
    shape = (8, peak.shape[1])
    row = lax.broadcasted_iota(jnp.int32, shape, 0)
    out = jnp.zeros(shape, F32)
    for i, part in enumerate(three_way(peak) + three_way(total)):
        out = jnp.where(row == i, jnp.broadcast_to(part, shape), out)
    return out


def attend_kernel(
    fill_ref, owner_ref, q_ref, k_hbm, v_hbm, nk_ref, nv_ref,
    ko_hbm, vo_hbm, out_ref, q_vmem, nk_vmem, nv_vmem, k_ref, v_ref, in_sem, k_sem, v_sem, ko_sem, vo_sem,
):
    steps, batch, width = q_ref.shape
    small = [
        pltpu.make_async_copy(src, dst, in_sem.at[i])
        for i, (src, dst) in enumerate(((q_ref, q_vmem), (nk_ref, nk_vmem), (nv_ref, nv_vmem)))
    ]
    for copy in small:
        copy.start()
    rows = k_ref.shape[1]
    heads = width // HD
    per_kv = heads // 2
    n = per_kv * steps * batch
    loads = []
    for b in range(batch):
        pair = (
            pltpu.make_async_copy(k_hbm.at[b], k_ref.at[b], k_sem.at[b]),
            pltpu.make_async_copy(v_hbm.at[b], v_ref.at[b], v_sem.at[b]),
        )
        pair[0].start()
        pair[1].start()
        loads.append(pair)

    me = lax.axis_index(CTX)
    lane = lax.broadcasted_iota(jnp.int32, (batch, rows), 1)
    sub = lax.broadcasted_iota(jnp.int32, (batch, rows), 0)
    live_steps = []
    slots = []
    seen = [jnp.int32(0)] * batch
    for s in range(steps):
        length = jnp.zeros((batch, rows), jnp.int32)
        for b in range(batch):
            mine = owner_ref[s, b] == me
            seen[b] = seen[b] + mine.astype(jnp.int32)
            end = fill_ref[0, b] + seen[b]
            slots.append((s, b, mine, end - 1))
            length = jnp.where(sub == b, end, length)
        live_steps.append(lane < length)
    live = jnp.concatenate(live_steps * per_kv, axis=0)

    for copy in small:
        copy.wait()
    q = q_vmem[...].astype(F32).reshape(steps * batch, width)
    q_groups = [
        jnp.concatenate([q[:, (g * per_kv + h) * HD : (g * per_kv + h + 1) * HD] for h in range(per_kv)], axis=0)
        for g in range(2)
    ]

    stores = []
    for b in range(batch):
        loads[b][0].wait()
        loads[b][1].wait()
        for s, sb, mine, slot in slots:
            if sb != b:
                continue

            @pl.when(mine)
            def _(s=s, slot=slot):
                base = pl.multiple_of((slot // 16) * 16, 16)
                at = lax.broadcasted_iota(jnp.int32, (16, 2 * HD), 0) == slot - base
                for ref, new in ((k_ref, nk_vmem), (v_ref, nv_vmem)):
                    old = ref[b, pl.ds(base, 16), :].astype(F32)
                    row = new[s, b : b + 1, :].astype(F32)
                    ref[b, pl.ds(base, 16), :] = jnp.where(at, jnp.broadcast_to(row, at.shape), old).astype(BF16)

        pair = (
            pltpu.make_async_copy(k_ref.at[b], ko_hbm.at[b], ko_sem.at[b]),
            pltpu.make_async_copy(v_ref.at[b], vo_hbm.at[b], vo_sem.at[b]),
        )
        pair[0].start()
        pair[1].start()
        stores.append(pair)

    which = lax.broadcasted_iota(jnp.int32, (n, HD), 0) % batch
    which_rows = lax.broadcasted_iota(jnp.int32, (n, rows), 0) % batch
    parts, stats = [], []
    for g in range(2):
        cols = slice(g * HD, (g + 1) * HD)
        scores = jnp.zeros((n, rows), F32)
        for p in range(0, batch, 2):
            lhs = jnp.concatenate(
                [jnp.where(which == p, q_groups[g], 0.0), jnp.where(which == p + 1, q_groups[g], 0.0)], axis=1
            ).astype(BF16)
            rhs = jnp.concatenate([k_ref[p, :, cols], k_ref[p + 1, :, cols]], axis=1)
            scores = scores + lax.dot_general(lhs, rhs, (((1,), (1,)), ((), ())), preferred_element_type=F32)
        masked = jnp.where(live, scores * (1.0 / HD**0.5), -1e30)
        peak = jnp.max(masked, axis=1, keepdims=True)
        weights = jnp.where(live, jnp.exp(masked - peak), 0.0)
        total = jnp.sum(weights, axis=1, keepdims=True)
        part = jnp.zeros((n, HD), F32)
        for b in range(batch):
            lhs = jnp.where(which_rows == b, weights, 0.0).astype(BF16)
            part = part + jnp.dot(lhs, v_ref[b, :, cols], preferred_element_type=F32)
        parts.append(part)
        col = lax.broadcasted_iota(jnp.int32, (n, HD), 1)
        stats.append(
            jnp.where(col == 0, jnp.broadcast_to(peak, (n, HD)), jnp.where(col == 1, jnp.broadcast_to(total, (n, HD)), 0.0))
        )
    part_t = jnp.concatenate(parts, axis=0).T
    stat_t = jnp.concatenate(stats, axis=0).T
    stat = stat_rows(stat_t[0:1], stat_t[1:2])
    dests = out_ref.shape[0]
    each = HD // dests
    for d in range(dests):
        out_ref[d] = jnp.concatenate([part_t[d * each : (d + 1) * each], stat], axis=0).astype(BF16)
    for pair in stores:
        pair[0].wait()
        pair[1].wait()


def combined(in_ref, each):
    x = in_ref[...].astype(F32)
    stat = x[:, each:]
    row = lax.broadcasted_iota(jnp.int32, stat.shape, 1)
    peak = jnp.sum(jnp.where(row < 3, stat, 0.0), axis=1, keepdims=True)
    total = jnp.sum(jnp.where((row >= 3) & (row < 6), stat, 0.0), axis=1, keepdims=True)
    top = jnp.max(peak, axis=0, keepdims=True)
    factor = jnp.exp(peak - top)
    return jnp.sum(x[:, :each] * factor, axis=0), top[0], jnp.sum(total * factor, axis=0)


def partial_kernel(in_ref, out_ref, *, each):
    part, top, total = combined(in_ref, each)
    block = jnp.concatenate([part, stat_rows(top, total)], axis=0).astype(BF16)
    for d in range(out_ref.shape[0]):
        out_ref[d] = block


def final_kernel(in_ref, out_ref, *, each):
    part, _, total = combined(in_ref, each)
    block = (part / total).astype(BF16)
    for d in range(out_ref.shape[0]):
        out_ref[d] = block


def project_kernel(in_ref, w_ref, out_ref):
    sources, each, n = in_ref.shape
    rows, cols = out_ref.shape[1], w_ref.shape[0]
    attention = in_ref[...].astype(F32).reshape(sources * each, n).T
    wide = jnp.concatenate([attention[h * rows : (h + 1) * rows] for h in range(n // rows)], axis=1)
    mixed = lax.dot_general(wide.astype(BF16), w_ref[...], (((1,), (1,)), ((), ())), preferred_element_type=F32)
    block = jnp.concatenate([mixed, jnp.zeros((rows, out_ref.shape[2] - cols), F32)], axis=1)
    for d in range(out_ref.shape[0]):
        out_ref[d] = block


def finish_kernel(in_ref, out_ref):
    steps, batch, cols = out_ref.shape
    x = in_ref[...]
    total = x[0]
    for d in range(1, x.shape[0]):
        total = total + x[d]
    me = lax.axis_index("head")
    mine = total[:, :cols]
    for d in range(1, x.shape[0]):
        mine = jnp.where(me == d, total[:, d * cols : (d + 1) * cols], mine)
    out_ref[...] = mine.reshape(steps, batch, cols).astype(BF16)


VMEM = pl.BlockSpec(memory_space=pltpu.VMEM)
SMEM = pl.BlockSpec(memory_space=pltpu.SMEM)
HBM = pl.BlockSpec(memory_space=pltpu.HBM)


def on_device(n_y, n_zc, n_head, queries, k_cache, v_cache, new_keys, new_values, fill, owner, out_weight):
    steps, batch, width = queries.shape
    rows = k_cache.shape[1]
    n = steps * batch * (width // HD)
    each = HD // n_zc
    struct = jax.ShapeDtypeStruct
    params = lambda mib: pltpu.CompilerParams(vmem_limit_bytes=mib * 2**20)
    keys_out, values_out, sent = pl.pallas_call(
        attend_kernel,
        out_shape=(
            struct(k_cache.shape, BF16),
            struct(v_cache.shape, BF16),
            struct((n_zc, each + 8, n), BF16),
        ),
        in_specs=[SMEM, SMEM, HBM, HBM, HBM, HBM, HBM],
        out_specs=(HBM, HBM, VMEM),
        scratch_shapes=[
            pltpu.VMEM(queries.shape, BF16),
            pltpu.VMEM(new_keys.shape, BF16),
            pltpu.VMEM(new_values.shape, BF16),
            pltpu.VMEM(k_cache.shape, BF16),
            pltpu.VMEM(v_cache.shape, BF16),
        ]
        + [pltpu.SemaphoreType.DMA((3,))]
        + [pltpu.SemaphoreType.DMA((batch,))] * 4,
        compiler_params=pltpu.CompilerParams(vmem_limit_bytes=ATTEND_VMEM),
        name="attend",
    )(fill.T, owner, queries, k_cache, v_cache, new_keys, new_values)
    got = lax.all_to_all(sent, ("z", "core"), 0, 0)
    sent = pl.pallas_call(
        functools.partial(partial_kernel, each=each),
        out_shape=struct((n_y, each + 8, n), BF16),
        in_specs=[VMEM],
        out_specs=VMEM,
        compiler_params=params(8),
        name="combine_zc",
    )(got)
    got = lax.all_to_all(sent, "y", 0, 0)
    sent = pl.pallas_call(
        functools.partial(final_kernel, each=each),
        out_shape=struct((n_zc, each, n), BF16),
        in_specs=[VMEM],
        out_specs=VMEM,
        compiler_params=params(8),
        name="combine_y",
    )(got)
    got = lax.all_to_all(sent, ("z", "core"), 0, 0)
    sent = pl.pallas_call(
        project_kernel,
        out_shape=struct((n_head, steps * batch, 128), F32),
        in_specs=[VMEM, VMEM],
        out_specs=VMEM,
        compiler_params=params(8),
        name="project",
    )(got, out_weight.T)
    got = lax.all_to_all(sent, "head", 0, 0)
    mixed = pl.pallas_call(
        finish_kernel,
        out_shape=struct((steps, batch, out_weight.shape[1] // n_head), BF16),
        in_specs=[VMEM],
        out_specs=VMEM,
        compiler_params=params(8),
        name="finish",
    )(got)
    return keys_out, values_out, mixed


def solution(mesh):
    n_ctx, n_head = mesh.devices.shape
    n_y, n_z = 8, n_ctx // 16
    split = Mesh(mesh.devices.reshape(n_y, n_z, 2, n_head), CTX + ("head",))
    in_specs = (
        P(None, None, "head"),
        P(None, CTX, "head"),
        P(None, CTX, "head"),
        P(None, None, "head"),
        P(None, None, "head"),
        P(None, CTX),
        P(),
        P("head", CTX),
    )
    out_specs = (P(None, CTX, "head"), P(None, CTX, "head"), P(None, None, CTX + ("head",)))
    return jax.shard_map(
        functools.partial(on_device, n_y, n_z * 2, n_head),
        mesh=split, in_specs=in_specs, out_specs=out_specs, check_vma=False,
    )
```

time: 1040 us -> 64.7 us (0.06)
  blocking collectives: 989 us -> 57.4 us
  waiting for transfers between devices: 21.8 us -> 0 us
  between operations: 14.2 us -> 0.66 us
    pmax x1 -> x0, blocking collectives: 498 us -> none  [on_device(): largest = lax.pmax(peak, 'ctx')]
    psum x1 -> x0, blocking collectives: 491 us -> none  [on_device(): lax.psum((numer * factor[..., None], total * factor), 'ctx')]
    all_to_all x0 -> x4, blocking collectives: none -> 57.4 us  [the longest x2 34.3 us: on_device(): got = lax.all_to_all(sent, ('z', 'core'), 0, 0)]
    reduce_scatter x1 -> x0, waiting for transfers between devices: 21.8 us -> none  [on_device(): lax.psum_scatter(partial_out, 'head', scatter_dimension=1, tiled=True)]
  transfers between devices with their start and end apart: 2 -> 0, of which waited for: 1 -> 0; matrix products, arithmetic and copies ran while one was open for 0% -> 0% of each run, Pallas kernels for 0% -> 0%
where the time goes in v1:
time: 64.7 us; the launch traced here: 64.3 us
  blocking collectives  57.4 us (89%)
  Pallas kernels  6.33 us (10%)
  between operations  0.66 us (1%)
    all_to_all x2, blocking collectives, on_device(): got = lax.all_to_all(sent, ('z', 'core'), 0, 0)  34.3 us
    all_to_all x1, blocking collectives, on_device(): got = lax.all_to_all(sent, 'y', 0, 0)  14.9 us
    all_to_all x1, blocking collectives, on_device(): got = lax.all_to_all(sent, 'head', 0, 0)  8.2 us
    pallas_call x1, Pallas kernels, on_device(): pl.pallas_call(attend_kernel, out_shape=(struct(k_cache.shape, BF16), str...  4.92 us

profile of v1, /device:TPU:1, one launch (start us, length us, event | category | flops | bytes accessed | tf_op | source)
XLA Modules:
  0.0 64.3 jit_solution(7805343774339560284)
XLA Ops:
  0.6 4.9 %attend.1 = (bf16[8,256,256]{2,1,0:T(8,128)(2,1)}, bf16[8,256,256]{2,1,0:T(8,128)(2,1)}, bf16[16,16,384]{2,1,0:T(8,128)(2,1)}) custom-call(s32[1,8]{1,0:T(1,128)} %bitcast.3, s32[3,8]{1,0:T(4,128)} %owner_ref.1, bf16[3,8,2048]{2,1,0:T(8,128)(2,1)} %q_ref.1, bf16[8,256,256]{2,1,0:T(8,128)(2,1)} %k_hbm.1, bf16[8,256,256]{2,1,0:T(8,128)(2,1)} %v_hbm.1, ...), custom_call_target="tpu_custom_call" | custom-call | tf_op jit(solution)/shard_map/attend/pallas_call | solution.py:207
  5.6 22.2 %all_to_all.20.in_ref = bf16[16,16,384]{2,1,0:T(8,128)(2,1)S(1)} all-to-all(bf16[16,16,384]{2,1,0:T(8,128)(2,1)} %get-tuple-element.8), channel_id=1, replica_groups=mesh['y'=8,'z'=8,'core'=2,'head'=4] {'z','core'}, dimensions={0} | all-to-all | bytes 393216 | tf_op jit(solution)/shard_map/all_to_all | solution.py:228
  27.7 0.2 combine_zc.1
  27.9 0.0 copy-start
  27.9 14.9 %all_to_all.21.in_ref = bf16[8,16,384]{2,1,0:T(8,128)(2,1)S(1)} all-to-all(bf16[8,16,384]{2,1,0:T(8,128)(2,1)S(1)} %combine_zc.1), channel_id=1, replica_groups=mesh['y'=8,'z'=8,'core'=2,'head'=4] {'y'}, dimensions={0} | all-to-all | bytes 196608 | tf_op jit(solution)/shard_map/all_to_all | solution.py:237
  42.8 0.1 combine_y.1
  42.9 12.1 %all_to_all.22.in_ref = bf16[16,8,384]{2,1,0:T(8,128)(2,1)S(1)} all-to-all(bf16[16,8,384]{2,1,0:T(8,128)(2,1)S(1)} %combine_y.1), channel_id=1, replica_groups=mesh['y'=8,'z'=8,'core'=2,'head'=4] {'z','core'}, dimensions={0} | all-to-all | bytes 196608 | tf_op jit(solution)/shard_map/all_to_all | solution.py:246
  55.0 0.0 copy-done
  55.0 0.3 project.1
  55.3 8.2 %all_to_all.23.in_ref = f32[4,24,128]{2,1,0:T(8,128)S(1)} all-to-all(f32[4,24,128]{2,1,0:T(8,128)S(1)} %project.1), channel_id=1, replica_groups=mesh['y'=8,'z'=8,'core'=2,'head'=4] {'head'}, dimensions={0} | all-to-all | bytes 98304 | tf_op jit(solution)/shard_map/all_to_all | solution.py:255
  63.5 0.9 %finish.1 = bf16[3,8,16]{2,1,0:T(8,128)(2,1)} custom-call(f32[4,24,128]{2,1,0:T(8,128)S(1)} %all_to_all.23.in_ref), custom_call_target="tpu_custom_call" | custom-call | tf_op jit(solution)/shard_map/finish/pallas_call | solution.py:256
Async XLA Ops:
  27.9 27.1 %copy-start = (bf16[2048,64]{0,1:T(8,128)(2,1)S(1)}, bf16[2048,64]{0,1:T(8,128)(2,1)}, u32[]{:S(2)}) copy-start(bf16[2048,64]{0,1:T(8,128)(2,1)} %param.15) | copy-start | bytes 786436

commit v2 on v1

v2 whole, which is shorter than its diff:
```python
import functools

import jax
import jax.numpy as jnp
from jax import lax
from jax.experimental import pallas as pl
from jax.experimental.pallas import tpu as pltpu
from jax.sharding import Mesh
from jax.sharding import PartitionSpec as P

HD = 128
F32 = jnp.float32
BF16 = jnp.bfloat16
ATTEND_VMEM = 63_000_000
CHUNKS = 2
CTX = ("y", "z", "core")


def three_way(x):
    first = x.astype(BF16).astype(F32)
    rest = x - first
    second = rest.astype(BF16).astype(F32)
    return first, second, rest - second


def attend_kernel(
    fill_hbm, owner_hbm, q_hbm, k_hbm, v_hbm, nk_hbm, nv_hbm,
    ko_hbm, vo_hbm, out_ref,
    fill_ref, owner_ref, q_ref, nk_ref, nv_ref, k_ref, v_ref, q_rows, rows_out, in_sem, load_sem, store_sem,
):
    steps, batch, width = q_ref.shape
    slots = k_ref.shape[1]
    heads = width // HD
    per_kv = heads // 2
    n = steps * heads
    size = batch // CHUNKS
    small = [
        pltpu.make_async_copy(src, dst, in_sem.at[i])
        for i, (src, dst) in enumerate(
            ((q_hbm, q_ref), (fill_hbm, fill_ref), (owner_hbm, owner_ref), (nk_hbm, nk_ref), (nv_hbm, nv_ref))
        )
    ]
    loads, stores = [], []
    for c in range(CHUNKS):
        part = pl.ds(c * size, size)
        for i, (hbm, vmem, out) in enumerate(((k_hbm, k_ref, ko_hbm), (v_hbm, v_ref, vo_hbm))):
            loads.append(pltpu.make_async_copy(hbm.at[part], vmem.at[part], load_sem.at[i, c]))
            stores.append(pltpu.make_async_copy(vmem.at[part], out.at[part], store_sem.at[i, c]))
    for copy in small + loads:
        copy.start()

    me = lax.axis_index(CTX)
    small[0].wait()
    q = q_ref[...].astype(F32)
    for s in range(steps):
        for h in range(heads):
            q_rows[:, s * heads + h, :] = q[s, :, h * HD : (h + 1) * HD]
    for copy in small[1:]:
        copy.wait()

    row = lax.broadcasted_iota(jnp.int32, (n, slots), 0)
    slot_id = lax.broadcasted_iota(jnp.int32, (n, slots), 1)
    lane = lax.broadcasted_iota(jnp.int32, (heads, HD), 1)
    peaks = jnp.zeros((heads, HD), F32)
    totals = jnp.zeros((heads, HD), F32)
    for c in range(CHUNKS):
        loads[2 * c].wait()
        loads[2 * c + 1].wait()
        ends = {}
        for b in range(c * size, (c + 1) * size):
            seen = jnp.int32(0)
            for s in range(steps):
                mine = owner_ref[s, b] == me
                seen = seen + mine.astype(jnp.int32)
                end = fill_ref[0, b] + seen
                ends[s, b] = end

                @pl.when(mine)
                def _(s=s, b=b, slot=end - 1):
                    base = pl.multiple_of((slot // 16) * 16, 16)
                    at = lax.broadcasted_iota(jnp.int32, (16, 2 * HD), 0) == slot - base
                    for ref, new in ((k_ref, nk_ref), (v_ref, nv_ref)):
                        old = ref[b, pl.ds(base, 16), :].astype(F32)
                        fresh = new[s, b : b + 1, :].astype(F32)
                        ref[b, pl.ds(base, 16), :] = jnp.where(at, jnp.broadcast_to(fresh, at.shape), old).astype(BF16)

        stores[2 * c].start()
        stores[2 * c + 1].start()
        for b in range(c * size, (c + 1) * size):
            length = jnp.where(row < heads, ends[0, b], ends[steps - 1, b])
            for s in range(1, steps - 1):
                length = jnp.where((row >= s * heads) & (row < (s + 1) * heads), ends[s, b], length)
            live = slot_id < length
            q_b = q_rows[b]
            first = (lax.broadcasted_iota(jnp.int32, (n, HD), 0) // per_kv) % 2 == 0
            lhs = jnp.concatenate([jnp.where(first, q_b, 0.0), jnp.where(first, 0.0, q_b)], axis=1).astype(BF16)
            scores = lax.dot_general(lhs, k_ref[b], (((1,), (1,)), ((), ())), preferred_element_type=F32)
            masked = jnp.where(live, scores * (1.0 / HD**0.5), -1e30)
            peak = jnp.max(masked, axis=1, keepdims=True)
            weights = jnp.where(live, jnp.exp(masked - peak), 0.0)
            total = jnp.sum(weights, axis=1, keepdims=True)
            both = jnp.dot(weights.astype(BF16), v_ref[b], preferred_element_type=F32)
            part = jnp.where(first, both[:, :HD], both[:, HD:])
            for s in range(steps):
                own = slice(s * heads, (s + 1) * heads)
                at = s * batch + b
                rows_out[:, at, :] = part[own]
                peaks = jnp.where(lane == at, peak[own], peaks)
                totals = jnp.where(lane == at, total[own], totals)
    used = steps * batch
    for i, piece in enumerate(three_way(peaks) + three_way(totals)):
        rows_out[:, used + i, :] = piece
    for i in range(6, 8):
        rows_out[:, used + i, :] = jnp.zeros((heads, HD), F32)
    for h in range(heads):
        out_ref[h] = rows_out[h].astype(BF16)
    for copy in stores:
        copy.wait()


def combined(in_ref):
    x = in_ref[...].astype(F32)
    used = x.shape[1] - 8
    stat = x[:, used:]
    row = lax.broadcasted_iota(jnp.int32, stat.shape, 1)
    peak = jnp.sum(jnp.where(row < 3, stat, 0.0), axis=1, keepdims=True)
    total = jnp.sum(jnp.where((row >= 3) & (row < 6), stat, 0.0), axis=1, keepdims=True)
    top = jnp.max(peak, axis=0, keepdims=True)
    factor = jnp.exp(peak - top)
    return x[:, :used], factor, top[0], jnp.sum(total * factor, axis=0)


def weighted(parts, factor):
    sources, rows, lanes = parts.shape
    shape = (1, rows, lanes)
    diagonal = lax.broadcasted_iota(jnp.int32, shape, 1) == lax.broadcasted_iota(jnp.int32, shape, 2)
    column = jnp.sum(jnp.where(diagonal, factor, 0.0), axis=2, keepdims=True)
    return jnp.sum(parts * column, axis=0)


def partial_kernel(in_ref, out_ref):
    parts, factor, top, total = combined(in_ref)
    row = lax.broadcasted_iota(jnp.int32, (8, HD), 0)
    stat = jnp.zeros((8, HD), F32)
    for i, piece in enumerate(three_way(top) + three_way(total)):
        stat = jnp.where(row == i, jnp.broadcast_to(piece, stat.shape), stat)
    block = jnp.concatenate([weighted(parts, factor), stat], axis=0).astype(BF16)
    for d in range(out_ref.shape[0]):
        out_ref[d] = block


def final_kernel(in_ref, out_ref):
    parts, factor, _, total = combined(in_ref)
    used = lax.broadcasted_iota(jnp.int32, total.shape, 1) < parts.shape[1]
    block = weighted(parts, factor / jnp.where(used, total, 1.0)[None]).astype(BF16)
    for d in range(out_ref.shape[0]):
        out_ref[d] = block


def project_kernel(in_ref, w_ref, out_ref):
    rows, cols = out_ref.shape[1], w_ref.shape[0]
    wide = jnp.concatenate([in_ref[h] for h in range(in_ref.shape[0])], axis=1)
    mixed = lax.dot_general(wide, w_ref[...], (((1,), (1,)), ((), ())), preferred_element_type=F32)
    block = jnp.concatenate([mixed, jnp.zeros((rows, out_ref.shape[2] - cols), F32)], axis=1)
    for d in range(out_ref.shape[0]):
        out_ref[d] = block


def finish_kernel(in_ref, out_ref):
    steps, batch, cols = out_ref.shape
    x = in_ref[...]
    total = x[0]
    for d in range(1, x.shape[0]):
        total = total + x[d]
    me = lax.axis_index("head")
    mine = total[:, :cols]
    for d in range(1, x.shape[0]):
        mine = jnp.where(me == d, total[:, d * cols : (d + 1) * cols], mine)
    out_ref[...] = mine.reshape(steps, batch, cols).astype(BF16)


VMEM = pl.BlockSpec(memory_space=pltpu.VMEM)
SMEM = pl.BlockSpec(memory_space=pltpu.SMEM)
HBM = pl.BlockSpec(memory_space=pltpu.HBM)


def on_device(n_y, n_zc, n_head, queries, k_cache, v_cache, new_keys, new_values, fill, owner, out_weight):
    steps, batch, width = queries.shape
    heads = width // HD
    used = steps * batch
    struct = jax.ShapeDtypeStruct
    params = lambda mib: pltpu.CompilerParams(vmem_limit_bytes=mib * 2**20)
    keys_out, values_out, sent = pl.pallas_call(
        attend_kernel,
        out_shape=(
            struct(k_cache.shape, BF16),
            struct(v_cache.shape, BF16),
            struct((n_zc, used + 8, HD), BF16),
        ),
        in_specs=[HBM] * 7,
        out_specs=(HBM, HBM, VMEM),
        scratch_shapes=[
            pltpu.SMEM((1, batch), jnp.int32),
            pltpu.SMEM(owner.shape, jnp.int32),
            pltpu.VMEM(queries.shape, BF16),
            pltpu.VMEM(new_keys.shape, BF16),
            pltpu.VMEM(new_values.shape, BF16),
            pltpu.VMEM(k_cache.shape, BF16),
            pltpu.VMEM(v_cache.shape, BF16),
            pltpu.VMEM((batch, steps * heads, HD), F32),
            pltpu.VMEM((heads, used + 8, HD), F32),
            pltpu.SemaphoreType.DMA((5,)),
            pltpu.SemaphoreType.DMA((2, CHUNKS)),
            pltpu.SemaphoreType.DMA((2, CHUNKS)),
        ],
        compiler_params=pltpu.CompilerParams(vmem_limit_bytes=ATTEND_VMEM),
        name="attend",
    )(fill.T, owner, queries, k_cache, v_cache, new_keys, new_values)
    got = lax.all_to_all(sent, ("z", "core"), 0, 0)
    sent = pl.pallas_call(
        partial_kernel,
        out_shape=struct((n_y, used + 8, HD), BF16),
        in_specs=[VMEM],
        out_specs=VMEM,
        compiler_params=params(8),
        name="combine_zc",
    )(got)
    got = lax.all_to_all(sent, "y", 0, 0)
    sent = pl.pallas_call(
        final_kernel,
        out_shape=struct((n_zc, used, HD), BF16),
        in_specs=[VMEM],
        out_specs=VMEM,
        compiler_params=params(8),
        name="combine_y",
    )(got)
    got = lax.all_to_all(sent, ("z", "core"), 0, 0)
    sent = pl.pallas_call(
        project_kernel,
        out_shape=struct((n_head, steps * batch, 128), F32),
        in_specs=[VMEM, VMEM],
        out_specs=VMEM,
        compiler_params=params(8),
        name="project",
    )(got, out_weight.T)
    got = lax.all_to_all(sent, "head", 0, 0)
    mixed = pl.pallas_call(
        finish_kernel,
        out_shape=struct((steps, batch, out_weight.shape[1] // n_head), BF16),
        in_specs=[VMEM],
        out_specs=VMEM,
        compiler_params=params(8),
        name="finish",
    )(got)
    return keys_out, values_out, mixed


def solution(mesh):
    n_ctx, n_head = mesh.devices.shape
    n_y, n_z = 8, n_ctx // 16
    split = Mesh(mesh.devices.reshape(n_y, n_z, 2, n_head), CTX + ("head",))
    in_specs = (
        P(None, None, "head"),
        P(None, CTX, "head"),
        P(None, CTX, "head"),
        P(None, None, "head"),
        P(None, None, "head"),
        P(None, CTX),
        P(),
        P("head", CTX),
    )
    out_specs = (P(None, CTX, "head"), P(None, CTX, "head"), P(None, None, CTX + ("head",)))
    return jax.shard_map(
        functools.partial(on_device, n_y, n_z * 2, n_head),
        mesh=split, in_specs=in_specs, out_specs=out_specs, check_vma=False,
    )
```

time: 64.7 us -> 62.5 us (0.966)
  blocking collectives: 57.4 us -> 55.5 us
    all_to_all x2, blocking collectives: 34.3 us -> 33.1 us  [on_device(): got = lax.all_to_all(sent, ('z', 'core'), 0, 0)]
    all_to_all x1, blocking collectives: 14.9 us -> 14.2 us  [on_device(): got = lax.all_to_all(sent, 'y', 0, 0)]
where the time goes in v2:
time: 62.5 us; the launch traced here: 62.1 us
  blocking collectives  55.5 us (89%)
  Pallas kernels  5.95 us (10%)
  between operations  0.67 us (1%)
    all_to_all x2, blocking collectives, on_device(): got = lax.all_to_all(sent, ('z', 'core'), 0, 0)  33.1 us
    all_to_all x1, blocking collectives, on_device(): got = lax.all_to_all(sent, 'y', 0, 0)  14.2 us
    all_to_all x1, blocking collectives, on_device(): got = lax.all_to_all(sent, 'head', 0, 0)  8.21 us
    pallas_call x1, Pallas kernels, on_device(): pl.pallas_call(attend_kernel, out_shape=(struct(k_cache.shape, BF16), str...  4.58 us

profile of v2, /device:TPU:1, one launch (start us, length us, event | category | flops | bytes accessed | tf_op | source)
XLA Modules:
  0.0 62.1 jit_solution(16549966582764676155)
XLA Ops:
  0.6 4.6 %attend.1 = (bf16[8,256,256]{2,1,0:T(8,128)(2,1)}, bf16[8,256,256]{2,1,0:T(8,128)(2,1)}, bf16[16,32,128]{2,1,0:T(8,128)(2,1)}) custom-call(s32[1,8]{1,0:T(1,128)} %bitcast.3, s32[3,8]{1,0:T(4,128)} %owner_hbm.1, bf16[3,8,2048]{2,1,0:T(8,128)(2,1)} %q_hbm.1, bf16[8,256,256]{2,1,0:T(8,128)(2,1)} %k_hbm.1, bf16[8,256,256]{2,1,0:T(8,128)(2,1)} %v_hbm.1, ...), custom_call_target="tpu_custom_call" | custom-call | tf_op jit(solution)/shard_map/attend/pallas_call | solution.py:193
  5.2 21.0 %all_to_all.20.in_ref = bf16[16,32,128]{2,1,0:T(8,128)(2,1)S(1)} all-to-all(bf16[16,32,128]{2,1,0:T(8,128)(2,1)} %get-tuple-element.8), channel_id=1, replica_groups=mesh['y'=8,'z'=8,'core'=2,'head'=4] {'z','core'}, dimensions={0} | all-to-all | bytes 262144 | tf_op jit(solution)/shard_map/all_to_all | solution.py:219
  26.2 0.2 combine_zc.1
  26.4 0.0 copy-start
  26.4 14.2 %all_to_all.21.in_ref = bf16[8,32,128]{2,1,0:T(8,128)(2,1)S(1)} all-to-all(bf16[8,32,128]{2,1,0:T(8,128)(2,1)S(1)} %combine_zc.1), channel_id=1, replica_groups=mesh['y'=8,'z'=8,'core'=2,'head'=4] {'y'}, dimensions={0} | all-to-all | bytes 131072 | tf_op jit(solution)/shard_map/all_to_all | solution.py:228
  40.6 0.1 combine_y.1
  40.7 12.1 %all_to_all.22.in_ref = bf16[16,24,128]{2,1,0:T(8,128)(2,1)S(1)} all-to-all(bf16[16,24,128]{2,1,0:T(8,128)(2,1)S(1)} %combine_y.1), channel_id=1, replica_groups=mesh['y'=8,'z'=8,'core'=2,'head'=4] {'z','core'}, dimensions={0} | all-to-all | bytes 196608 | tf_op jit(solution)/shard_map/all_to_all | solution.py:237
  52.9 0.0 copy-done
  52.9 0.2 project.1
  53.1 8.2 %all_to_all.23.in_ref = f32[4,24,128]{2,1,0:T(8,128)S(1)} all-to-all(f32[4,24,128]{2,1,0:T(8,128)S(1)} %project.1), channel_id=1, replica_groups=mesh['y'=8,'z'=8,'core'=2,'head'=4] {'head'}, dimensions={0} | all-to-all | bytes 98304 | tf_op jit(solution)/shard_map/all_to_all | solution.py:246
  61.3 0.9 %finish.1 = bf16[3,8,16]{2,1,0:T(8,128)(2,1)} custom-call(f32[4,24,128]{2,1,0:T(8,128)S(1)} %all_to_all.23.in_ref), custom_call_target="tpu_custom_call" | custom-call | tf_op jit(solution)/shard_map/finish/pallas_call | solution.py:247
Async XLA Ops:
  26.4 26.5 %copy-start = (bf16[2048,64]{0,1:T(8,128)(2,1)S(1)}, bf16[2048,64]{0,1:T(8,128)(2,1)}, u32[]{:S(2)}) copy-start(bf16[2048,64]{0,1:T(8,128)(2,1)} %param.15) | copy-start | bytes 786436

commit v3 on v2

v3 whole, which is shorter than its diff:
```python
import functools

import jax
import jax.numpy as jnp
from jax import lax
from jax.experimental import pallas as pl
from jax.experimental.pallas import tpu as pltpu
from jax.sharding import Mesh
from jax.sharding import PartitionSpec as P

HD = 128
F32 = jnp.float32
BF16 = jnp.bfloat16
ATTEND_VMEM = 63_000_000
CHUNKS = 2
CTX = ("y2", "y1", "y0", "z2", "z1", "z0", "core")
HEAD = ("x1", "x0")
SPREAD = ("core", "z2", "z1", "z0")
GATHER = ("core", "z2", "z1", "z0")
MERGE = ('y0', 'y1', 'y2')
LAST = ("x1", "x0")


def three_way(x):
    first = x.astype(BF16).astype(F32)
    rest = x - first
    second = rest.astype(BF16).astype(F32)
    return first, second, rest - second


def attend_kernel(
    fill_hbm, owner_hbm, q_hbm, k_hbm, v_hbm, nk_hbm, nv_hbm,
    ko_hbm, vo_hbm, out_ref,
    fill_ref, owner_ref, q_ref, nk_ref, nv_ref, k_ref, v_ref, q_rows, s_rows, rows_out, in_sem, load_sem, store_sem,
):
    steps, batch, width = q_ref.shape
    slots = k_ref.shape[1]
    heads = width // HD
    per_kv = heads // 2
    n = steps * heads
    size = batch // CHUNKS
    small = [
        pltpu.make_async_copy(src, dst, in_sem.at[i])
        for i, (src, dst) in enumerate(
            ((q_hbm, q_ref), (fill_hbm, fill_ref), (owner_hbm, owner_ref), (nk_hbm, nk_ref), (nv_hbm, nv_ref))
        )
    ]
    loads, stores = [[], []], [[], []]
    for i, (hbm, vmem, out) in enumerate(((k_hbm, k_ref, ko_hbm), (v_hbm, v_ref, vo_hbm))):
        for c in range(CHUNKS):
            part = pl.ds(c * size, size)
            loads[i].append(pltpu.make_async_copy(hbm.at[part], vmem.at[part], load_sem.at[i, c]))
            stores[i].append(pltpu.make_async_copy(vmem.at[part], out.at[part], store_sem.at[i, c]))
    for copy in small + loads[0] + loads[1]:
        copy.start()

    me = lax.axis_index(CTX)
    small[0].wait()
    q = q_ref[...].astype(F32)
    for s in range(steps):
        for h in range(heads):
            q_rows[:, s * heads + h, :] = q[s, :, h * HD : (h + 1) * HD]
    for copy in small[1:]:
        copy.wait()

    mine, ends = {}, {}
    for b in range(batch):
        end = fill_ref[0, b]
        for s in range(steps):
            mine[s, b] = owner_ref[s, b] == me
            end = end + mine[s, b].astype(jnp.int32)
            ends[s, b] = end

    def append(ref, new, b):
        for s in range(steps):

            @pl.when(mine[s, b])
            def _(s=s, slot=ends[s, b] - 1):
                base = pl.multiple_of((slot // 16) * 16, 16)
                at = lax.broadcasted_iota(jnp.int32, (16, 2 * HD), 0) == slot - base
                old = ref[b, pl.ds(base, 16), :].astype(F32)
                fresh = new[s, b : b + 1, :].astype(F32)
                ref[b, pl.ds(base, 16), :] = jnp.where(at, jnp.broadcast_to(fresh, at.shape), old).astype(BF16)

    row = lax.broadcasted_iota(jnp.int32, (n, slots), 0)
    slot_id = lax.broadcasted_iota(jnp.int32, (n, slots), 1)
    lane = lax.broadcasted_iota(jnp.int32, (heads, HD), 1)
    first = (lax.broadcasted_iota(jnp.int32, (n, HD), 0) // per_kv) % 2 == 0
    peaks = jnp.zeros((heads, HD), F32)
    totals = jnp.zeros((heads, HD), F32)
    gap = jnp.zeros((n, 2 * HD), BF16)
    rest = jnp.zeros((HD - 2 * n, 2 * HD), BF16)
    for c in range(CHUNKS):
        loads[0][c].wait()
        for b in range(c * size, (c + 1) * size):
            append(k_ref, nk_ref, b)
        stores[0][c].start()
    for pair in range(0, batch, 2):
        scores_t = jnp.zeros((slots, HD), F32)
        for b in (pair, pair + 1):
            q_b = q_rows[b]
            own = jnp.concatenate([jnp.where(first, q_b, 0.0), jnp.where(first, 0.0, q_b)], axis=1).astype(BF16)
            rhs = jnp.concatenate([own, gap, rest] if b == pair else [gap, own, rest], axis=0)
            scores_t = scores_t + lax.dot_general(
                k_ref[b], rhs, (((1,), (1,)), ((), ())), preferred_element_type=F32
            )
        s_rows[pair // 2] = scores_t.T
    for c in range(CHUNKS):
        loads[1][c].wait()
        for b in range(c * size, (c + 1) * size):
            append(v_ref, nv_ref, b)
        stores[1][c].start()
    for b in range(batch):
        length = jnp.where(row < heads, ends[0, b], ends[steps - 1, b])
        for s in range(1, steps - 1):
            length = jnp.where((row >= s * heads) & (row < (s + 1) * heads), ends[s, b], length)
        live = slot_id < length
        scores = s_rows[b // 2, (b % 2) * n : (b % 2 + 1) * n, :]
        masked = jnp.where(live, scores * (1.0 / HD**0.5), -1e30)
        peak = jnp.max(masked, axis=1, keepdims=True)
        weights = jnp.where(live, jnp.exp(masked - peak), 0.0)
        total = jnp.sum(weights, axis=1, keepdims=True)
        both = jnp.dot(weights.astype(BF16), v_ref[b], preferred_element_type=F32)
        part = jnp.where(first, both[:, :HD], both[:, HD:])
        for s in range(steps):
            own = slice(s * heads, (s + 1) * heads)
            at = s * batch + b
            rows_out[:, at, :] = part[own]
            peaks = jnp.where(lane == at, peak[own], peaks)
            totals = jnp.where(lane == at, total[own], totals)
    used = steps * batch
    for i, piece in enumerate(three_way(peaks) + three_way(totals)):
        rows_out[:, used + i, :] = piece
    for i in range(6, 8):
        rows_out[:, used + i, :] = jnp.zeros((heads, HD), F32)
    for h in range(heads):
        out_ref[h] = rows_out[h].astype(BF16)
    for copy in stores[0] + stores[1]:
        copy.wait()


def combined(in_ref):
    x = in_ref[...].astype(F32)
    used = x.shape[1] - 8
    stat = x[:, used:]
    row = lax.broadcasted_iota(jnp.int32, stat.shape, 1)
    peak = jnp.sum(jnp.where(row < 3, stat, 0.0), axis=1, keepdims=True)
    total = jnp.sum(jnp.where((row >= 3) & (row < 6), stat, 0.0), axis=1, keepdims=True)
    top = jnp.max(peak, axis=0, keepdims=True)
    factor = jnp.exp(peak - top)
    return x[:, :used], factor, top[0], jnp.sum(total * factor, axis=0)


def weighted(parts, factor):
    sources, rows, lanes = parts.shape
    shape = (1, rows, lanes)
    diagonal = lax.broadcasted_iota(jnp.int32, shape, 1) == lax.broadcasted_iota(jnp.int32, shape, 2)
    column = jnp.sum(jnp.where(diagonal, factor, 0.0), axis=2, keepdims=True)
    return jnp.sum(parts * column, axis=0)


def partial_kernel(in_ref, out_ref):
    parts, factor, top, total = combined(in_ref)
    row = lax.broadcasted_iota(jnp.int32, (8, HD), 0)
    stat = jnp.zeros((8, HD), F32)
    for i, piece in enumerate(three_way(top) + three_way(total)):
        stat = jnp.where(row == i, jnp.broadcast_to(piece, stat.shape), stat)
    block = jnp.concatenate([weighted(parts, factor), stat], axis=0).astype(BF16)
    for d in range(out_ref.shape[0]):
        out_ref[d] = block


def final_kernel(in_ref, out_ref):
    parts, factor, _, total = combined(in_ref)
    used = lax.broadcasted_iota(jnp.int32, total.shape, 1) < parts.shape[1]
    block = weighted(parts, factor / jnp.where(used, total, 1.0)[None]).astype(BF16)
    for d in range(out_ref.shape[0]):
        out_ref[d] = block


def place(index, order, wanted):
    bits = {axis: index >> (len(order) - 1 - i) & 1 for i, axis in enumerate(order)}
    return sum(bits[axis] << (len(wanted) - 1 - i) for i, axis in enumerate(wanted))


def project_kernel(in_ref, w_ref, out_ref):
    dests, batch, lanes = out_ref.shape
    steps = in_ref.shape[1] // batch
    each = w_ref.shape[0] // dests
    wide = jnp.concatenate([in_ref[place(h, SPREAD, GATHER)] for h in range(in_ref.shape[0])], axis=1)
    mixed = lax.dot_general(wide, w_ref[...], (((1,), (1,)), ((), ())), preferred_element_type=F32)
    rest = jnp.zeros((batch, lanes - steps * each), F32)
    for d in range(dests):
        pieces = [mixed[s * batch : (s + 1) * batch, d * each : (d + 1) * each] for s in range(steps)]
        out_ref[place(d, HEAD, LAST)] = jnp.concatenate(pieces + [rest], axis=1)


def finish_kernel(in_ref, out_ref):
    steps, batch, cols = out_ref.shape
    total = in_ref[0]
    for d in range(1, in_ref.shape[0]):
        total = total + in_ref[d]
    for s in range(steps):
        out_ref[s] = total[:, s * cols : (s + 1) * cols].astype(BF16)


VMEM = pl.BlockSpec(memory_space=pltpu.VMEM)
SMEM = pl.BlockSpec(memory_space=pltpu.SMEM)
HBM = pl.BlockSpec(memory_space=pltpu.HBM)


def on_device(n_y, n_zc, n_head, queries, k_cache, v_cache, new_keys, new_values, fill, owner, out_weight):
    steps, batch, width = queries.shape
    heads = width // HD
    used = steps * batch
    struct = jax.ShapeDtypeStruct
    params = lambda mib: pltpu.CompilerParams(vmem_limit_bytes=mib * 2**20)
    keys_out, values_out, sent = pl.pallas_call(
        attend_kernel,
        out_shape=(
            struct(k_cache.shape, BF16),
            struct(v_cache.shape, BF16),
            struct((n_zc, used + 8, HD), BF16),
        ),
        in_specs=[HBM] * 7,
        out_specs=(HBM, HBM, VMEM),
        scratch_shapes=[
            pltpu.SMEM((1, batch), jnp.int32),
            pltpu.SMEM(owner.shape, jnp.int32),
            pltpu.VMEM(queries.shape, BF16),
            pltpu.VMEM(new_keys.shape, BF16),
            pltpu.VMEM(new_values.shape, BF16),
            pltpu.VMEM(k_cache.shape, BF16),
            pltpu.VMEM(v_cache.shape, BF16),
            pltpu.VMEM((batch, steps * heads, HD), F32),
            pltpu.VMEM((batch // 2, HD, k_cache.shape[1]), F32),
            pltpu.VMEM((heads, used + 8, HD), F32),
            pltpu.SemaphoreType.DMA((5,)),
            pltpu.SemaphoreType.DMA((2, CHUNKS)),
            pltpu.SemaphoreType.DMA((2, CHUNKS)),
        ],
        compiler_params=pltpu.CompilerParams(vmem_limit_bytes=ATTEND_VMEM),
        name="attend",
    )(fill.T, owner, queries, k_cache, v_cache, new_keys, new_values)
    got = lax.all_to_all(sent, SPREAD, 0, 0)
    sent = pl.pallas_call(
        partial_kernel,
        out_shape=struct((n_y, used + 8, HD), BF16),
        in_specs=[VMEM],
        out_specs=VMEM,
        compiler_params=params(8),
        name="combine_zc",
    )(got)
    got = lax.all_to_all(sent, MERGE, 0, 0)
    sent = pl.pallas_call(
        final_kernel,
        out_shape=struct((n_zc, used, HD), BF16),
        in_specs=[VMEM],
        out_specs=VMEM,
        compiler_params=params(8),
        name="combine_y",
    )(got)
    got = lax.all_to_all(sent, GATHER, 0, 0)
    sent = pl.pallas_call(
        project_kernel,
        out_shape=struct((n_head, batch, 128), F32),
        in_specs=[VMEM, VMEM],
        out_specs=VMEM,
        compiler_params=params(8),
        name="project",
    )(got, out_weight.T)
    got = lax.all_to_all(sent, LAST, 0, 0)
    mixed = pl.pallas_call(
        finish_kernel,
        out_shape=struct((steps, batch, out_weight.shape[1] // n_head), BF16),
        in_specs=[VMEM],
        out_specs=VMEM,
        compiler_params=params(8),
        name="finish",
    )(got)
    return keys_out, values_out, mixed


def solution(mesh):
    split = Mesh(mesh.devices.reshape((2,) * 9), CTX + HEAD)
    in_specs = (
        P(None, None, HEAD),
        P(None, CTX, HEAD),
        P(None, CTX, HEAD),
        P(None, None, HEAD),
        P(None, None, HEAD),
        P(None, CTX),
        P(),
        P(HEAD, CTX),
    )
    out_specs = (P(None, CTX, HEAD), P(None, CTX, HEAD), P(None, None, CTX + HEAD))
    return jax.shard_map(
        functools.partial(on_device, 2 ** len(MERGE), 2 ** len(SPREAD), 2 ** len(HEAD)),
        mesh=split, in_specs=in_specs, out_specs=out_specs, check_vma=False,
    )
```

time: 62.5 us -> 59.8 us (0.957)
  blocking collectives: 55.5 us -> 53.7 us
  Pallas kernels: 5.95 us -> 4.85 us
    all_to_all x4, blocking collectives: 55.5 us -> 53.7 us  [the longest x1 19.1 us: on_device(): got = lax.all_to_all(sent, SPREAD, 0, 0)]
    pallas_call x1, Pallas kernels: 4.58 us -> 3.63 us  [on_device(): pl.pallas_call(attend_kernel, out_shape=(struct(k_cache.shape, BF16), str...]
where the time goes in v3:
time: 59.8 us; the launch traced here: 59.2 us
  blocking collectives  53.7 us (90%)
  Pallas kernels  4.85 us (8%)
  between operations  0.67 us (1%)
    all_to_all x1, blocking collectives, on_device(): got = lax.all_to_all(sent, SPREAD, 0, 0)  19.1 us
    all_to_all x1, blocking collectives, on_device(): got = lax.all_to_all(sent, MERGE, 0, 0)  13.5 us
    all_to_all x1, blocking collectives, on_device(): got = lax.all_to_all(sent, GATHER, 0, 0)  13.1 us
    all_to_all x1, blocking collectives, on_device(): got = lax.all_to_all(sent, LAST, 0, 0)  8.04 us
    pallas_call x1, Pallas kernels, on_device(): pl.pallas_call(attend_kernel, out_shape=(struct(k_cache.shape, BF16), str...  3.63 us

profile of v3, /device:TPU:1, one launch (start us, length us, event | category | flops | bytes accessed | tf_op | source)
XLA Modules:
  0.0 59.2 jit_solution(12387567291744766006)
XLA Ops:
  0.6 3.6 %attend.1 = (bf16[8,256,256]{2,1,0:T(8,128)(2,1)}, bf16[8,256,256]{2,1,0:T(8,128)(2,1)}, bf16[16,32,128]{2,1,0:T(8,128)(2,1)}) custom-call(s32[1,8]{1,0:T(1,128)} %bitcast.3, s32[3,8]{1,0:T(4,128)} %owner_hbm.1, bf16[3,8,2048]{2,1,0:T(8,128)(2,1)} %q_hbm.1, bf16[8,256,256]{2,1,0:T(8,128)(2,1)} %k_hbm.1, bf16[8,256,256]{2,1,0:T(8,128)(2,1)} %v_hbm.1, ...), custom_call_target="tpu_custom_call" | custom-call | tf_op jit(solution)/shard_map/attend/pallas_call | solution.py:218
  4.3 19.1 %all_to_all.20.in_ref = bf16[16,32,128]{2,1,0:T(8,128)(2,1)S(1)} all-to-all(bf16[16,32,128]{2,1,0:T(8,128)(2,1)} %get-tuple-element.8), channel_id=1, replica_groups=mesh['y2'=2,'y1'=2,'y0'=2,'z2'=2,'z1'=2,'z0'=2,'core'=2,'x1'=2,'x0'=2] {..., dimensions={0} | all-to-all | bytes 262144 | tf_op jit(solution)/shard_map/all_to_all | solution.py:245
  23.4 0.2 combine_zc.1
  23.6 0.0 copy-start
  23.6 13.5 %all_to_all.21.in_ref = bf16[8,32,128]{2,1,0:T(8,128)(2,1)S(1)} all-to-all(bf16[8,32,128]{2,1,0:T(8,128)(2,1)S(1)} %combine_zc.1), channel_id=1, replica_groups=mesh['y2'=2,'y1'=2,'y0'=2,'z2'=2,'z1'=2,'z0'=2,'core'=2,'x1'=2,'x0'=2] {..., dimensions={0} | all-to-all | bytes 131072 | tf_op jit(solution)/shard_map/all_to_all | solution.py:254
  37.0 0.1 combine_y.1
  37.2 13.1 %all_to_all.22.in_ref = bf16[16,24,128]{2,1,0:T(8,128)(2,1)S(1)} all-to-all(bf16[16,24,128]{2,1,0:T(8,128)(2,1)S(1)} %combine_y.1), channel_id=1, replica_groups=mesh['y2'=2,'y1'=2,'y0'=2,'z2'=2,'z1'=2,'z0'=2,'core'=2,'x1'=2,'x0'=2] {..., dimensions={0} | all-to-all | bytes 196608 | tf_op jit(solution)/shard_map/all_to_all | solution.py:263
  50.3 0.0 copy-done
  50.3 0.3 project.1
  50.5 8.0 %all_to_all.23.in_ref = f32[4,8,128]{2,1,0:T(8,128)S(1)} all-to-all(f32[4,8,128]{2,1,0:T(8,128)S(1)} %project.1), channel_id=1, replica_groups=mesh['y2'=2,'y1'=2,'y0'=2,'z2'=2,'z1'=2,'z0'=2,'core'=2,'x1'=2,'x0'=2] {..., dimensions={0} | all-to-all | bytes 32768 | tf_op jit(solution)/shard_map/all_to_all | solution.py:272
  58.6 0.7 %finish.1 = bf16[3,8,16]{2,1,0:T(8,128)(2,1)} custom-call(f32[4,8,128]{2,1,0:T(8,128)S(1)} %all_to_all.23.in_ref), custom_call_target="tpu_custom_call" | custom-call | tf_op jit(solution)/shard_map/finish/pallas_call | solution.py:273
Async XLA Ops:
  23.6 26.7 %copy-start = (bf16[2048,64]{0,1:T(8,128)(2,1)S(1)}, bf16[2048,64]{0,1:T(8,128)(2,1)}, u32[]{:S(2)}) copy-start(bf16[2048,64]{0,1:T(8,128)(2,1)} %param.15) | copy-start | bytes 786436

commit v4 on v3

--- a/solution.py
+++ b/solution.py
@@ -12,7 +12,7 @@
 F32 = jnp.float32
 BF16 = jnp.bfloat16
 ATTEND_VMEM = 63_000_000
-CHUNKS = 2
+CHUNKS = 1
 CTX = ("y2", "y1", "y0", "z2", "z1", "z0", "core")
 HEAD = ("x1", "x0")
 SPREAD = ("core", "z2", "z1", "z0")
@@ -30,8 +30,8 @@
 
 def attend_kernel(
     fill_hbm, owner_hbm, q_hbm, k_hbm, v_hbm, nk_hbm, nv_hbm,
-    ko_hbm, vo_hbm, out_ref,
-    fill_ref, owner_ref, q_ref, nk_ref, nv_ref, k_ref, v_ref, q_rows, s_rows, rows_out, in_sem, load_sem, store_sem,
+    ko_hbm, vo_hbm, out_hbm,
+    fill_ref, owner_ref, q_ref, nk_ref, nv_ref, k_ref, v_ref, q_rows, s_rows, rows_out, out_ref, in_sem, load_sem, store_sem, out_sem,
 ):
     steps, batch, width = q_ref.shape
     slots = k_ref.shape[1]
@@ -135,7 +135,9 @@
         rows_out[:, used + i, :] = jnp.zeros((heads, HD), F32)
     for h in range(heads):
         out_ref[h] = rows_out[h].astype(BF16)
-    for copy in stores[0] + stores[1]:
+    sent = pltpu.make_async_copy(out_ref, out_hbm, out_sem)
+    sent.start()
+    for copy in stores[0] + stores[1] + [sent]:
         copy.wait()
 
 
@@ -223,7 +225,7 @@
             struct((n_zc, used + 8, HD), BF16),
         ),
         in_specs=[HBM] * 7,
-        out_specs=(HBM, HBM, VMEM),
+        out_specs=(HBM, HBM, HBM),
         scratch_shapes=[
             pltpu.SMEM((1, batch), jnp.int32),
             pltpu.SMEM(owner.shape, jnp.int32),
@@ -235,9 +237,11 @@
             pltpu.VMEM((batch, steps * heads, HD), F32),
             pltpu.VMEM((batch // 2, HD, k_cache.shape[1]), F32),
             pltpu.VMEM((heads, used + 8, HD), F32),
+            pltpu.VMEM((n_zc, used + 8, HD), BF16),
             pltpu.SemaphoreType.DMA((5,)),
             pltpu.SemaphoreType.DMA((2, CHUNKS)),
             pltpu.SemaphoreType.DMA((2, CHUNKS)),
+            pltpu.SemaphoreType.DMA,
         ],
         compiler_params=pltpu.CompilerParams(vmem_limit_bytes=ATTEND_VMEM),
         name="attend",

time: 59.8 us -> 59.3 us (level)
  no operation moved by 1% of the time
where the time goes in v4:
time: 59.3 us; the launch traced here: 58.7 us
  blocking collectives  53.6 us (90%)
  Pallas kernels  4.38 us (7%)
  between operations  0.67 us (1%)
    all_to_all x1, blocking collectives, on_device(): got = lax.all_to_all(sent, SPREAD, 0, 0)  19.1 us
    all_to_all x1, blocking collectives, on_device(): got = lax.all_to_all(sent, MERGE, 0, 0)  13.4 us
    all_to_all x1, blocking collectives, on_device(): got = lax.all_to_all(sent, GATHER, 0, 0)  13.1 us
    all_to_all x1, blocking collectives, on_device(): got = lax.all_to_all(sent, LAST, 0, 0)  8.04 us
    pallas_call x1, Pallas kernels, on_device(): pl.pallas_call(attend_kernel, out_shape=(struct(k_cache.shape, BF16), str...  3.16 us

profile of v4, /device:TPU:1, one launch (start us, length us, event | category | flops | bytes accessed | tf_op | source)
XLA Modules:
  0.0 58.7 jit_solution(6239365268306677810)
XLA Ops:
  0.6 3.2 %attend.1 = (bf16[8,256,256]{2,1,0:T(8,128)(2,1)}, bf16[8,256,256]{2,1,0:T(8,128)(2,1)}, bf16[16,32,128]{2,1,0:T(8,128)(2,1)}) custom-call(s32[1,8]{1,0:T(1,128)} %bitcast.3, s32[3,8]{1,0:T(4,128)} %owner_hbm.1, bf16[3,8,2048]{2,1,0:T(8,128)(2,1)} %q_hbm.1, bf16[8,256,256]{2,1,0:T(8,128)(2,1)} %k_hbm.1, bf16[8,256,256]{2,1,0:T(8,128)(2,1)} %v_hbm.1, ...), custom_call_target="tpu_custom_call" | custom-call | tf_op jit(solution)/shard_map/attend/pallas_call | solution.py:220
  3.8 19.1 %all_to_all.20.in_ref = bf16[16,32,128]{2,1,0:T(8,128)(2,1)S(1)} all-to-all(bf16[16,32,128]{2,1,0:T(8,128)(2,1)} %get-tuple-element.8), channel_id=1, replica_groups=mesh['y2'=2,'y1'=2,'y0'=2,'z2'=2,'z1'=2,'z0'=2,'core'=2,'x1'=2,'x0'=2] {..., dimensions={0} | all-to-all | bytes 262144 | tf_op jit(solution)/shard_map/all_to_all | solution.py:249
  22.9 0.2 combine_zc.1
  23.1 0.0 copy-start
  23.1 13.4 %all_to_all.21.in_ref = bf16[8,32,128]{2,1,0:T(8,128)(2,1)S(1)} all-to-all(bf16[8,32,128]{2,1,0:T(8,128)(2,1)S(1)} %combine_zc.1), channel_id=1, replica_groups=mesh['y2'=2,'y1'=2,'y0'=2,'z2'=2,'z1'=2,'z0'=2,'core'=2,'x1'=2,'x0'=2] {..., dimensions={0} | all-to-all | bytes 131072 | tf_op jit(solution)/shard_map/all_to_all | solution.py:258
  36.5 0.1 combine_y.1
  36.6 13.1 %all_to_all.22.in_ref = bf16[16,24,128]{2,1,0:T(8,128)(2,1)S(1)} all-to-all(bf16[16,24,128]{2,1,0:T(8,128)(2,1)S(1)} %combine_y.1), channel_id=1, replica_groups=mesh['y2'=2,'y1'=2,'y0'=2,'z2'=2,'z1'=2,'z0'=2,'core'=2,'x1'=2,'x0'=2] {..., dimensions={0} | all-to-all | bytes 196608 | tf_op jit(solution)/shard_map/all_to_all | solution.py:267
  49.7 0.0 copy-done
  49.7 0.3 project.1
  50.0 8.0 %all_to_all.23.in_ref = f32[4,8,128]{2,1,0:T(8,128)S(1)} all-to-all(f32[4,8,128]{2,1,0:T(8,128)S(1)} %project.1), channel_id=1, replica_groups=mesh['y2'=2,'y1'=2,'y0'=2,'z2'=2,'z1'=2,'z0'=2,'core'=2,'x1'=2,'x0'=2] {..., dimensions={0} | all-to-all | bytes 32768 | tf_op jit(solution)/shard_map/all_to_all | solution.py:276
  58.0 0.7 %finish.1 = bf16[3,8,16]{2,1,0:T(8,128)(2,1)} custom-call(f32[4,8,128]{2,1,0:T(8,128)S(1)} %all_to_all.23.in_ref), custom_call_target="tpu_custom_call" | custom-call | tf_op jit(solution)/shard_map/finish/pallas_call | solution.py:277
Async XLA Ops:
  23.1 26.6 %copy-start = (bf16[2048,64]{0,1:T(8,128)(2,1)S(1)}, bf16[2048,64]{0,1:T(8,128)(2,1)}, u32[]{:S(2)}) copy-start(bf16[2048,64]{0,1:T(8,128)(2,1)} %param.15) | copy-start | bytes 786436

commit v5 on v4

--- a/solution.py
+++ b/solution.py
@@ -12,7 +12,6 @@
 F32 = jnp.float32
 BF16 = jnp.bfloat16
 ATTEND_VMEM = 63_000_000
-CHUNKS = 1
 CTX = ("y2", "y1", "y0", "z2", "z1", "z0", "core")
 HEAD = ("x1", "x0")
 SPREAD = ("core", "z2", "z1", "z0")
@@ -38,20 +37,17 @@
     heads = width // HD
     per_kv = heads // 2
     n = steps * heads
-    size = batch // CHUNKS
     small = [
         pltpu.make_async_copy(src, dst, in_sem.at[i])
         for i, (src, dst) in enumerate(
             ((q_hbm, q_ref), (fill_hbm, fill_ref), (owner_hbm, owner_ref), (nk_hbm, nk_ref), (nv_hbm, nv_ref))
         )
     ]
-    loads, stores = [[], []], [[], []]
+    loads, stores = [], []
     for i, (hbm, vmem, out) in enumerate(((k_hbm, k_ref, ko_hbm), (v_hbm, v_ref, vo_hbm))):
-        for c in range(CHUNKS):
-            part = pl.ds(c * size, size)
-            loads[i].append(pltpu.make_async_copy(hbm.at[part], vmem.at[part], load_sem.at[i, c]))
-            stores[i].append(pltpu.make_async_copy(vmem.at[part], out.at[part], store_sem.at[i, c]))
-    for copy in small + loads[0] + loads[1]:
+        loads.append(pltpu.make_async_copy(hbm, vmem, load_sem.at[i]))
+        stores.append(pltpu.make_async_copy(vmem, out, store_sem.at[i]))
+    for copy in small + loads:
         copy.start()
 
     me = lax.axis_index(CTX)
@@ -90,11 +86,15 @@
     totals = jnp.zeros((heads, HD), F32)
     gap = jnp.zeros((n, 2 * HD), BF16)
     rest = jnp.zeros((HD - 2 * n, 2 * HD), BF16)
-    for c in range(CHUNKS):
-        loads[0][c].wait()
-        for b in range(c * size, (c + 1) * size):
+    some = functools.reduce(jnp.logical_or, mine.values())
+    loads[0].wait()
+
+    @pl.when(some)
+    def _():
+        for b in range(batch):
             append(k_ref, nk_ref, b)
-        stores[0][c].start()
+
+    stores[0].start()
     for pair in range(0, batch, 2):
         scores_t = jnp.zeros((slots, HD), F32)
         for b in (pair, pair + 1):
@@ -105,11 +105,14 @@
                 k_ref[b], rhs, (((1,), (1,)), ((), ())), preferred_element_type=F32
             )
         s_rows[pair // 2] = scores_t.T
-    for c in range(CHUNKS):
-        loads[1][c].wait()
-        for b in range(c * size, (c + 1) * size):
+    loads[1].wait()
+
+    @pl.when(some)
+    def _():
+        for b in range(batch):
             append(v_ref, nv_ref, b)
-        stores[1][c].start()
+
+    stores[1].start()
     for b in range(batch):
         length = jnp.where(row < heads, ends[0, b], ends[steps - 1, b])
         for s in range(1, steps - 1):
@@ -137,7 +140,7 @@
         out_ref[h] = rows_out[h].astype(BF16)
     sent = pltpu.make_async_copy(out_ref, out_hbm, out_sem)
     sent.start()
-    for copy in stores[0] + stores[1] + [sent]:
+    for copy in stores + [sent]:
         copy.wait()
 
 
@@ -239,8 +242,8 @@
             pltpu.VMEM((heads, used + 8, HD), F32),
             pltpu.VMEM((n_zc, used + 8, HD), BF16),
             pltpu.SemaphoreType.DMA((5,)),
-            pltpu.SemaphoreType.DMA((2, CHUNKS)),
-            pltpu.SemaphoreType.DMA((2, CHUNKS)),
+            pltpu.SemaphoreType.DMA((2,)),
+            pltpu.SemaphoreType.DMA((2,)),
             pltpu.SemaphoreType.DMA,
         ],
         compiler_params=pltpu.CompilerParams(vmem_limit_bytes=ATTEND_VMEM),

time: 59.3 us -> 59.2 us (level)
  no operation moved by 1% of the time
where the time goes in v5:
time: 59.2 us; the launch traced here: 58.7 us
  blocking collectives  53.6 us (91%)
  Pallas kernels  4.37 us (7%)
  between operations  0.67 us (1%)
    all_to_all x1, blocking collectives, on_device(): got = lax.all_to_all(sent, SPREAD, 0, 0)  19 us
    all_to_all x1, blocking collectives, on_device(): got = lax.all_to_all(sent, MERGE, 0, 0)  13.5 us
    all_to_all x1, blocking collectives, on_device(): got = lax.all_to_all(sent, GATHER, 0, 0)  13.1 us
    all_to_all x1, blocking collectives, on_device(): got = lax.all_to_all(sent, LAST, 0, 0)  8.03 us
    pallas_call x1, Pallas kernels, on_device(): pl.pallas_call(attend_kernel, out_shape=(struct(k_cache.shape, BF16), str...  3.15 us

profile of v5, /device:TPU:1, one launch (start us, length us, event | category | flops | bytes accessed | tf_op | source)
XLA Modules:
  0.0 58.7 jit_solution(7743346118844876213)
XLA Ops:
  0.6 3.1 %attend.1 = (bf16[8,256,256]{2,1,0:T(8,128)(2,1)}, bf16[8,256,256]{2,1,0:T(8,128)(2,1)}, bf16[16,32,128]{2,1,0:T(8,128)(2,1)}) custom-call(s32[1,8]{1,0:T(1,128)} %bitcast.3, s32[3,8]{1,0:T(4,128)} %owner_hbm.1, bf16[3,8,2048]{2,1,0:T(8,128)(2,1)} %q_hbm.1, bf16[8,256,256]{2,1,0:T(8,128)(2,1)} %k_hbm.1, bf16[8,256,256]{2,1,0:T(8,128)(2,1)} %v_hbm.1, ...), custom_call_target="tpu_custom_call" | custom-call | tf_op jit(solution)/shard_map/attend/pallas_call | solution.py:223
  3.8 19.0 %all_to_all.20.in_ref = bf16[16,32,128]{2,1,0:T(8,128)(2,1)S(1)} all-to-all(bf16[16,32,128]{2,1,0:T(8,128)(2,1)} %get-tuple-element.8), channel_id=1, replica_groups=mesh['y2'=2,'y1'=2,'y0'=2,'z2'=2,'z1'=2,'z0'=2,'core'=2,'x1'=2,'x0'=2] {..., dimensions={0} | all-to-all | bytes 262144 | tf_op jit(solution)/shard_map/all_to_all | solution.py:252
  22.8 0.2 combine_zc.1
  23.0 0.0 copy-start
  23.0 13.5 %all_to_all.21.in_ref = bf16[8,32,128]{2,1,0:T(8,128)(2,1)S(1)} all-to-all(bf16[8,32,128]{2,1,0:T(8,128)(2,1)S(1)} %combine_zc.1), channel_id=1, replica_groups=mesh['y2'=2,'y1'=2,'y0'=2,'z2'=2,'z1'=2,'z0'=2,'core'=2,'x1'=2,'x0'=2] {..., dimensions={0} | all-to-all | bytes 131072 | tf_op jit(solution)/shard_map/all_to_all | solution.py:261
  36.5 0.1 combine_y.1
  36.6 13.1 %all_to_all.22.in_ref = bf16[16,24,128]{2,1,0:T(8,128)(2,1)S(1)} all-to-all(bf16[16,24,128]{2,1,0:T(8,128)(2,1)S(1)} %combine_y.1), channel_id=1, replica_groups=mesh['y2'=2,'y1'=2,'y0'=2,'z2'=2,'z1'=2,'z0'=2,'core'=2,'x1'=2,'x0'=2] {..., dimensions={0} | all-to-all | bytes 196608 | tf_op jit(solution)/shard_map/all_to_all | solution.py:270
  49.7 0.0 copy-done
  49.7 0.3 project.1
  50.0 8.0 %all_to_all.23.in_ref = f32[4,8,128]{2,1,0:T(8,128)S(1)} all-to-all(f32[4,8,128]{2,1,0:T(8,128)S(1)} %project.1), channel_id=1, replica_groups=mesh['y2'=2,'y1'=2,'y0'=2,'z2'=2,'z1'=2,'z0'=2,'core'=2,'x1'=2,'x0'=2] {..., dimensions={0} | all-to-all | bytes 32768 | tf_op jit(solution)/shard_map/all_to_all | solution.py:279
  58.0 0.7 %finish.1 = bf16[3,8,16]{2,1,0:T(8,128)(2,1)} custom-call(f32[4,8,128]{2,1,0:T(8,128)S(1)} %all_to_all.23.in_ref), custom_call_target="tpu_custom_call" | custom-call | tf_op jit(solution)/shard_map/finish/pallas_call | solution.py:280
Async XLA Ops:
  23.0 26.8 %copy-start = (bf16[2048,64]{0,1:T(8,128)(2,1)S(1)}, bf16[2048,64]{0,1:T(8,128)(2,1)}, u32[]{:S(2)}) copy-start(bf16[2048,64]{0,1:T(8,128)(2,1)} %param.15) | copy-start | bytes 786436

commit v6 on v5

--- a/solution.py
+++ b/solution.py
@@ -14,8 +14,8 @@
 ATTEND_VMEM = 63_000_000
 CTX = ("y2", "y1", "y0", "z2", "z1", "z0", "core")
 HEAD = ("x1", "x0")
-SPREAD = ("core", "z2", "z1", "z0")
-GATHER = ("core", "z2", "z1", "z0")
+SPREAD = ("core", "z1", "z2", "z0")
+GATHER = ("core", "z1", "z2", "z0")
 MERGE = ('y0', 'y1', 'y2')
 LAST = ("x1", "x0")
 

time: 59.2 us -> 59.1 us (level)
  no operation moved by 1% of the time
where the time goes in v6:
time: 59.1 us; the launch traced here: 58.6 us
  blocking collectives  53.7 us (91%)
  Pallas kernels  4.24 us (7%)
  between operations  0.67 us (1%)
    all_to_all x1, blocking collectives, on_device(): got = lax.all_to_all(sent, SPREAD, 0, 0)  19.5 us
    all_to_all x1, blocking collectives, on_device(): got = lax.all_to_all(sent, MERGE, 0, 0)  13.4 us
    all_to_all x1, blocking collectives, on_device(): got = lax.all_to_all(sent, GATHER, 0, 0)  12.7 us
    all_to_all x1, blocking collectives, on_device(): got = lax.all_to_all(sent, LAST, 0, 0)  8.03 us
    pallas_call x1, Pallas kernels, on_device(): pl.pallas_call(attend_kernel, out_shape=(struct(k_cache.shape, BF16), str...  3.02 us

profile of v6, /device:TPU:1, one launch (start us, length us, event | category | flops | bytes accessed | tf_op | source)
XLA Modules:
  0.0 58.6 jit_solution(8206736542661685666)
XLA Ops:
  0.6 3.0 %attend.1 = (bf16[8,256,256]{2,1,0:T(8,128)(2,1)}, bf16[8,256,256]{2,1,0:T(8,128)(2,1)}, bf16[16,32,128]{2,1,0:T(8,128)(2,1)}) custom-call(s32[1,8]{1,0:T(1,128)} %bitcast.3, s32[3,8]{1,0:T(4,128)} %owner_hbm.1, bf16[3,8,2048]{2,1,0:T(8,128)(2,1)} %q_hbm.1, bf16[8,256,256]{2,1,0:T(8,128)(2,1)} %k_hbm.1, bf16[8,256,256]{2,1,0:T(8,128)(2,1)} %v_hbm.1, ...), custom_call_target="tpu_custom_call" | custom-call | tf_op jit(solution)/shard_map/attend/pallas_call | solution.py:223
  3.7 19.5 %all_to_all.20.in_ref = bf16[16,32,128]{2,1,0:T(8,128)(2,1)S(1)} all-to-all(bf16[16,32,128]{2,1,0:T(8,128)(2,1)} %get-tuple-element.8), channel_id=1, replica_groups=mesh['y2'=2,'y1'=2,'y0'=2,'z2'=2,'z1'=2,'z0'=2,'core'=2,'x1'=2,'x0'=2] {..., dimensions={0} | all-to-all | bytes 262144 | tf_op jit(solution)/shard_map/all_to_all | solution.py:252
  23.2 0.2 combine_zc.1
  23.4 0.0 copy-start
  23.4 13.4 %all_to_all.21.in_ref = bf16[8,32,128]{2,1,0:T(8,128)(2,1)S(1)} all-to-all(bf16[8,32,128]{2,1,0:T(8,128)(2,1)S(1)} %combine_zc.1), channel_id=1, replica_groups=mesh['y2'=2,'y1'=2,'y0'=2,'z2'=2,'z1'=2,'z0'=2,'core'=2,'x1'=2,'x0'=2] {..., dimensions={0} | all-to-all | bytes 131072 | tf_op jit(solution)/shard_map/all_to_all | solution.py:261
  36.8 0.1 combine_y.1
  36.9 12.7 %all_to_all.22.in_ref = bf16[16,24,128]{2,1,0:T(8,128)(2,1)S(1)} all-to-all(bf16[16,24,128]{2,1,0:T(8,128)(2,1)S(1)} %combine_y.1), channel_id=1, replica_groups=mesh['y2'=2,'y1'=2,'y0'=2,'z2'=2,'z1'=2,'z0'=2,'core'=2,'x1'=2,'x0'=2] {..., dimensions={0} | all-to-all | bytes 196608 | tf_op jit(solution)/shard_map/all_to_all | solution.py:270
  49.6 0.0 copy-done
  49.6 0.3 project.1
  49.9 8.0 %all_to_all.23.in_ref = f32[4,8,128]{2,1,0:T(8,128)S(1)} all-to-all(f32[4,8,128]{2,1,0:T(8,128)S(1)} %project.1), channel_id=1, replica_groups=mesh['y2'=2,'y1'=2,'y0'=2,'z2'=2,'z1'=2,'z0'=2,'core'=2,'x1'=2,'x0'=2] {..., dimensions={0} | all-to-all | bytes 32768 | tf_op jit(solution)/shard_map/all_to_all | solution.py:279
  57.9 0.7 %finish.1 = bf16[3,8,16]{2,1,0:T(8,128)(2,1)} custom-call(f32[4,8,128]{2,1,0:T(8,128)S(1)} %all_to_all.23.in_ref), custom_call_target="tpu_custom_call" | custom-call | tf_op jit(solution)/shard_map/finish/pallas_call | solution.py:280
Async XLA Ops:
  23.4 26.3 %copy-start = (bf16[2048,64]{0,1:T(8,128)(2,1)S(1)}, bf16[2048,64]{0,1:T(8,128)(2,1)}, u32[]{:S(2)}) copy-start(bf16[2048,64]{0,1:T(8,128)(2,1)} %param.15) | copy-start | bytes 786436
